TPU v7x, 32 devices: a whole 2x2x4 slice. The times are simulated.
32 devices in a mesh: tm: 16 (over z, y, x), panel: 2 (over core).
Axes of the slice: x: 2, y: 2, z: 4, core: 2. Of those that a mesh axis runs over, the one named last changes fastest.
Arguments:
- factor_inverse: float32 [16, 768, 768], P('tm', None, 'panel'), may hold values from -1 to 1, as said below
- coupling: float32 [16, 768, 768], P('tm', None, 'panel'), may hold values from -1 to 1
- sigma_after: float32 [768, 768], replicated, may hold values from -1 to 3, as said below
Outputs:
- marginal_cov: float32 [16, 768, 768], P('tm', None, 'panel')
- propagator: bfloat16 [16, 768, 768], P('tm', None, 'panel')
Inputs may be any that keep to these rules, and one draw needn't show every extreme that they name: `factor_inverse`: factor_inverse_t is lower triangular with a positive diagonal. sigma_after is symmetric.
All inputs are finite; a program needn't handle non-finite values.
Results may differ from a plain program's by a relative error of at most 0.007.
The roundings to bfloat16 on the way count: a program that leaves them out, or rounds other values in their place, can miss the bound.
Values may be sent and summed in bfloat16 or wider, within the bound.
No kernel may reach another device: no remote copies, remote signals or barrier semaphores. Data moves between devices by JAX's collectives and lax.ppermute only.
A program may use at most 64 MiB of HBM per device.

v0:
```python
import jax
import jax.numpy as jnp
from jax import lax
from jax.sharding import PartitionSpec as P


def passed_along(block, axis, distance):
    devices = range(lax.axis_size(axis))
    route = [(i - distance, i) for i in devices if i - distance in devices]
    return lax.ppermute(block, axis, route)


def shards(factor_inverse, coupling, sigma_after):
    highest = lax.Precision.HIGHEST
    steps_tm = lax.axis_size("tm")
    where_tm = lax.axis_index("tm")
    panel_width = factor_inverse.shape[2]
    panel_start = lax.axis_index("panel") * panel_width
    factor_cols = factor_inverse[0]
    base_cols = lax.dot_general(
        lax.all_gather(factor_cols.astype(jnp.bfloat16), "panel", axis=1, tiled=True).astype(
            jnp.float32
        ),
        factor_cols,
        (((0,), (0,)), ((), ())),
        precision=highest,
        preferred_element_type=jnp.float32,
    )
    own_part = coupling[0].astype(jnp.bfloat16)
    full_coupling = lax.all_gather(own_part, "panel", axis=1, tiled=True)
    is_last = where_tm == steps_tm - 1
    exact_coupling = full_coupling.astype(jnp.float32)
    weighted = jnp.dot(sigma_after, own_part.astype(jnp.float32), precision=highest)
    folded = lax.dot_general(exact_coupling, weighted, (((0,), (0,)), ((), ())), precision=highest)
    covariance = base_cols + jnp.where(is_last, folded, jnp.zeros_like(folded))
    composite = full_coupling
    final_cols = own_part
    rounds = (steps_tm - 1).bit_length()
    for round_bit in range(rounds):
        distance = 1 << round_bit
        keep_going = round_bit + 1 < rounds
        share_bf = covariance.astype(jnp.bfloat16)
        own_cols = lax.dynamic_slice_in_dim(composite, panel_start, panel_width, 1)
        incoming = passed_along(share_bf, "tm", -distance)
        partner_comp = passed_along(composite, "tm", -distance)
        partner_cov = lax.all_gather(incoming, "panel", axis=1, tiled=True)
        middle = jnp.dot(partner_cov, own_cols, preferred_element_type=jnp.float32).astype(
            jnp.bfloat16
        )
        update = lax.dot_general(
            composite, middle, (((0,), (0,)), ((), ())), preferred_element_type=jnp.float32
        )
        active = where_tm + distance < steps_tm
        covariance = jnp.where(active, covariance + update, covariance)
        if keep_going:
            extended_complement = jnp.dot(
                partner_comp, composite, preferred_element_type=jnp.float32
            ).astype(jnp.bfloat16)
            composite = jnp.where(active, extended_complement, composite)
        else:
            extended_cols = jnp.dot(
                partner_comp, own_cols, preferred_element_type=jnp.float32
            ).astype(jnp.bfloat16)
            final_cols = jnp.where(active, extended_cols, own_cols)
    return (covariance[None], final_cols[None])


def solution(mesh):
    placed = (P("tm", None, "panel"), P("tm", None, "panel"), P())
    return jax.shard_map(
        shards,
        mesh=mesh,
        in_specs=placed,
        out_specs=(P("tm", None, "panel"), P("tm", None, "panel")),
        check_vma=False,
    )
```

profile of v0, /device:TPU:0, one launch (start us, length us, event | category | flops | bytes accessed | tf_op | source)
XLA Modules:
  0.0 284.7 jit_solution(2808531228455342037)
XLA Ops:
  7.2 2.3 bitcast_convert_fusion
  10.6 4.2 %fusion.12 = f32[768,384]{1,0:T(8,128)} fusion(f32[768,768]{1,0:T(8,128)S(1)} %copy-done, bf16[1,768,384]{2,1,0:T(8,128)(2,1)} %convert_element_type.49), kind=kOutput, calls=%fused_computation.26 | convolution fusion | flops 2717908992 | bytes 4128768 | tf_op jit(solution)/shard_map/dot_general | solution.py:33
  14.8 7.3 %all-gather.8.cloned.1.call-done = bf16[768,768]{1,0:T(8,128)(2,1)} async-done(((bf16[768,384]{1,0:T(8,128)(2,1)}), bf16[768,768]{1,0:T(8,128)(2,1)}) %all-gather.8.cloned.1.call-update) | async-done | bytes 1179664 | tf_op jit(solution)/shard_map/all_gather | solution.py:21
  22.1 4.3 %fusion.8 = f32[768,384]{1,0:T(8,128)} fusion(bf16[768,768]{1,0:T(8,128)(2,1)} %all-gather.8.cloned.1.call-done, f32[1,768,384]{2,1,0:T(8,128)S(1)} %copy-done.1), kind=kOutput, calls=%fused_computation.22 | convolution fusion | flops 2717908992 | bytes 3538944 | tf_op jit(solution)/shard_map/dot_general | solution.py:20
  26.4 7.6 %all-gather.18.cloned.1.call-done = bf16[1,768,768]{2,1,0:T(8,128)(2,1)} async-done(((bf16[1,768,384]{2,1,0:T(8,128)(2,1)}), bf16[1,768,768]{2,1,0:T(8,128)(2,1)}) %all-gather.18.cloned.1.call-update) | async-done | bytes 1179664 | tf_op jit(solution)/shard_map/all_gather | solution.py:30
  34.0 5.1 %fusion.35 = (bf16[768,384]{1,0:T(8,128)(2,1)S(1)}, f32[768,384]{1,0:T(8,128)}) fusion(f32[768,384]{1,0:T(8,128)} %fusion.8, f32[768,384]{1,0:T(8,128)} %fusion.12, bf16[1,768,768]{2,1,0:T(8,128)(2,1)} %all-gather.18.cloned.1.call-done, pred[]{:T(512)S(6)} %eq.3), kind=kOutput, calls=%fused_computation.41 | convolution fusion | flops 2718793728 | bytes 5308417 | tf_op jit(solution)/shard_map/dot_general | solution.py:34
  39.2 1.3 collective-permute-start
  40.5 16.2 %collective-permute-done = bf16[768,384]{1,0:T(8,128)(2,1)} collective-permute-done((bf16[768,384]{1,0:T(8,128)(2,1)S(1)}, bf16[768,384]{1,0:T(8,128)(2,1)}, u32[]{:S(2)}, u32[]{:S(2)}) %collective-permute-start) | collective-permute-done | bytes 589856 | tf_op jit(solution)/shard_map/ppermute | solution.py:10
  56.8 11.4 %all-gather.10.cloned.1.call-done = bf16[768,768]{1,0:T(8,128)(2,1)} async-done(((bf16[768,384]{1,0:T(8,128)(2,1)}), bf16[768,768]{1,0:T(8,128)(2,1)}) %all-gather.10.cloned.1.call-update) | async-done | bytes 1179664 | tf_op jit(solution)/shard_map/all_gather | solution.py:46
  68.1 4.2 %fusion.36 = (bf16[768,384]{1,0:T(8,128)(2,1)}, f32[768,384]{1,0:T(8,128)}) fusion(f32[768,384]{1,0:T(8,128)} %get-tuple-element.3, bf16[1,768,768]{2,1,0:T(8,128)(2,1)S(1)} %copy-done.3, bf16[768,768]{1,0:T(8,128)(2,1)} %all-gather.10.cloned.1.call-done, s32[]{:T(128)S(6)} %select_n.74, pred[]{:T(512)S(6)} %lt.21), kind=kOutput, calls=%fused_computation.42 | convolution fusion | flops 907149312 | bytes 5898245 | tf_op jit(solution)/shard_map/dot_general | solution.py:50
  72.3 1.3 collective-permute-start.2
  73.6 1.3 collective-permute-start.1
  74.9 15.1 %collective-permute-done.2 = bf16[768,384]{1,0:T(8,128)(2,1)} collective-permute-done((bf16[768,384]{1,0:T(8,128)(2,1)}, bf16[768,384]{1,0:T(8,128)(2,1)}, u32[]{:S(2)}, u32[]{:S(2)}) %collective-permute-start.2) | collective-permute-done | bytes 589856 | tf_op jit(solution)/shard_map/ppermute | solution.py:10
  90.2 13.6 %collective-permute-done.1 = bf16[768,768]{1,0:T(8,128)(2,1)} collective-permute-done((bf16[768,768]{1,0:T(8,128)(2,1)S(1)}, bf16[768,768]{1,0:T(8,128)(2,1)}, u32[]{:S(2)}, u32[]{:S(2)}) %collective-permute-start.1) | collective-permute-done | bytes 1179680 | tf_op jit(solution)/shard_map/ppermute | solution.py:10
  103.8 3.4 %fusion = bf16[768,768]{1,0:T(8,128)(2,1)} fusion(bf16[768,768]{1,0:T(8,128)(2,1)} %collective-permute-done.1, pred[]{:T(512)S(6)} %lt.21, bf16[1,768,768]{2,1,0:T(8,128)(2,1)S(1)} %copy-done.3), kind=kOutput, calls=%fused_computation.7 | convolution fusion | flops 907149312 | bytes 3538945 | tf_op jit(solution)/shard_map/dot_general | solution.py:56
  107.2 1.3 collective-permute-start.3
  108.5 16.5 %all-gather.12.cloned.1.call-done = bf16[768,768]{1,0:T(8,128)(2,1)} async-done(((bf16[768,384]{1,0:T(8,128)(2,1)}), bf16[768,768]{1,0:T(8,128)(2,1)}) %all-gather.12.cloned.1.call-update) | async-done | bytes 1179664 | tf_op jit(solution)/shard_map/all_gather | solution.py:46
  125.0 4.6 %fusion.39 = (bf16[768,384]{1,0:T(8,128)(2,1)S(1)}, f32[768,384]{1,0:T(8,128)}) fusion(f32[768,384]{1,0:T(8,128)} %get-tuple-element.5, bf16[768,768]{1,0:T(8,128)(2,1)} %fusion, bf16[768,768]{1,0:T(8,128)(2,1)} %all-gather.12.cloned.1.call-done, s32[]{:T(128)S(6)} %select_n.74, pred[]{:T(512)S(6)} %lt.20), kind=kOutput, calls=%fused_computation.43 | convolution fusion | flops 907149312 | bytes 5898245 | tf_op jit(solution)/shard_map/dot_general | solution.py:50
  129.6 1.3 collective-permute-start.4
  130.9 28.9 %collective-permute-done.4 = bf16[768,384]{1,0:T(8,128)(2,1)S(1)} collective-permute-done((bf16[768,384]{1,0:T(8,128)(2,1)S(1)}, bf16[768,384]{1,0:T(8,128)(2,1)S(1)}, u32[]{:S(2)}, u32[]{:S(2)}) %collective-permute-start.4) | collective-permute-done | bytes 589856 | tf_op jit(solution)/shard_map/ppermute | solution.py:10
  160.6 4.1 %fusion.1 = bf16[768,768]{1,0:T(8,128)(2,1)} fusion(bf16[768,768]{1,0:T(8,128)(2,1)} %fusion, bf16[768,768]{1,0:T(8,128)(2,1)} %collective-permute-done.3, pred[]{:T(512)S(6)} %lt.20), kind=kOutput, calls=%fused_computation.8 | convolution fusion | flops 907149312 | bytes 3538945 | tf_op jit(solution)/shard_map/dot_general | solution.py:56
  164.7 1.5 collective-permute-start.5
  166.2 6.0 %all-gather.14.cloned.1.call-done = bf16[768,768]{1,0:T(8,128)(2,1)} async-done(((bf16[768,384]{1,0:T(8,128)(2,1)}), bf16[768,768]{1,0:T(8,128)(2,1)}) %all-gather.14.cloned.1.call-update) | async-done | bytes 1179664 | tf_op jit(solution)/shard_map/all_gather | solution.py:46
  172.2 4.6 %fusion.42 = (bf16[768,384]{1,0:T(8,128)(2,1)S(1)}, f32[768,384]{1,0:T(8,128)}) fusion(f32[768,384]{1,0:T(8,128)} %get-tuple-element.7, bf16[768,768]{1,0:T(8,128)(2,1)} %fusion.1, bf16[768,768]{1,0:T(8,128)(2,1)} %all-gather.14.cloned.1.call-done, s32[]{:T(128)S(6)} %select_n.74, pred[]{:T(512)S(6)} %lt.19), kind=kOutput, calls=%fused_computation.44 | convolution fusion | flops 907149312 | bytes 5898245 | tf_op jit(solution)/shard_map/dot_general | solution.py:50
  176.8 1.3 collective-permute-start.6
  178.0 16.4 %collective-permute-done.5 = bf16[768,768]{1,0:T(8,128)(2,1)} collective-permute-done((bf16[768,768]{1,0:T(8,128)(2,1)}, bf16[768,768]{1,0:T(8,128)(2,1)}, u32[]{:S(2)}, u32[]{:S(2)}) %collective-permute-start.5) | collective-permute-done | bytes 1179680 | tf_op jit(solution)/shard_map/ppermute | solution.py:10
  194.4 4.1 %fusion.2 = bf16[768,768]{1,0:T(8,128)(2,1)} fusion(bf16[768,768]{1,0:T(8,128)(2,1)} %fusion.1, bf16[768,768]{1,0:T(8,128)(2,1)} %collective-permute-done.5, pred[]{:T(512)S(6)} %lt.19), kind=kOutput, calls=%fused_computation.9 | convolution fusion | flops 907149312 | bytes 3538945 | tf_op jit(solution)/shard_map/dot_general | solution.py:56
  198.5 1.3 collective-permute-start.7
  199.8 47.4 %collective-permute-done.6 = bf16[768,384]{1,0:T(8,128)(2,1)S(1)} collective-permute-done((bf16[768,384]{1,0:T(8,128)(2,1)S(1)}, bf16[768,384]{1,0:T(8,128)(2,1)S(1)}, u32[]{:S(2)}, u32[]{:S(2)}) %collective-permute-start.6) | collective-permute-done | bytes 589856 | tf_op jit(solution)/shard_map/ppermute | solution.py:10
  248.0 22.4 %collective-permute-done.7 = bf16[768,768]{1,0:T(8,128)(2,1)} collective-permute-done((bf16[768,768]{1,0:T(8,128)(2,1)}, bf16[768,768]{1,0:T(8,128)(2,1)}, u32[]{:S(2)}, u32[]{:S(2)}) %collective-permute-start.7) | collective-permute-done | bytes 1179680 | tf_op jit(solution)/shard_map/ppermute | solution.py:10
  270.5 3.2 %fusion.7 = bf16[1,768,384]{2,1,0:T(8,128)(2,1)} fusion(bf16[768,768]{1,0:T(8,128)(2,1)} %collective-permute-done.7, pred[]{:T(512)S(6)} %lt.18, bf16[768,768]{1,0:T(8,128)(2,1)} %fusion.2, s32[]{:T(128)S(6)} %select_n.74), kind=kOutput, calls=%fused_computation.21 | convolution fusion | flops 453574656 | bytes 2950656 | tf_op jit(solution)/shard_map/dot_general | solution.py:61
  273.7 4.2 %fusion.5 = f32[1,768,384]{2,1,0:T(8,128)} fusion(f32[768,384]{1,0:T(8,128)S(1)} %copy-done.6, bf16[768,768]{1,0:T(8,128)(2,1)} %fusion.2, bf16[768,768]{1,0:T(8,128)(2,1)} %all-gather.16.cloned.1.call-done, pred[]{:T(512)S(6)} %lt.18, s32[]{:T(128)S(6)} %select_n.74), kind=kOutput, calls=%fused_computation.14 | convolution fusion | flops 906854400 | bytes 5308421 | tf_op jit(solution)/shard_map/dot_general | solution.py:50
  (29 shorter events, 2.9 us)
Async XLA Ops:
  7.2 3.5 %copy-start = (f32[768,768]{1,0:T(8,128)S(1)}, f32[768,768]{1,0:T(8,128)}, u32[]{:S(2)}) copy-start(f32[768,768]{1,0:T(8,128)} %param.5) | copy-start | bytes 7077892
  7.2 2.5 copy-start.2
  7.2 14.9 %all-gather.8.cloned.1.call-start = ((), (), s32[]{:S(2)}) async-start(), calls=%async_computation | async-start | bytes 1769472 | tf_op jit(solution)/shard_map/all_gather | solution.py:21
  9.6 24.4 %all-gather.18.cloned.1.call-start = ((), (), s32[]{:S(2)}) async-start(), calls=%async_computation.5 | async-start | bytes 1769472 | tf_op jit(solution)/shard_map/all_gather | solution.py:30
  10.6 57.6 %all-gather.10.cloned.1.call-start = ((), (), s32[]{:S(2)}) async-start(), calls=%async_computation.1 | async-start | bytes 1769472 | tf_op jit(solution)/shard_map/all_gather | solution.py:46
  10.6 11.5 %copy-start.1 = (f32[1,768,384]{2,1,0:T(8,128)S(1)}, f32[1,768,384]{2,1,0:T(8,128)}, u32[]{:S(2)}) copy-start(f32[1,768,384]{2,1,0:T(8,128)} %param.3) | copy-start | bytes 3538948
  34.0 34.1 %copy-start.3 = (bf16[1,768,768]{2,1,0:T(8,128)(2,1)S(1)}, bf16[1,768,768]{2,1,0:T(8,128)(2,1)}, u32[]{:S(2)}) copy-start(bf16[1,768,768]{2,1,0:T(8,128)(2,1)} %all-gather.18.cloned.1.call-done) | copy-start | bytes 3538948
  39.2 17.5 %collective-permute-start = (bf16[768,384]{1,0:T(8,128)(2,1)S(1)}, bf16[768,384]{1,0:T(8,128)(2,1)}, u32[]{:S(2)}, u32[]{:S(2)}) collective-permute-start(bf16[768,384]{1,0:T(8,128)(2,1)S(1)} %get-tuple-element.2), channel_id=1, source_target_pairs={{2,0},{4,2},{6,4},{8,6},{10,8},{12,10},{14,12},{16,14},{18,16},{20... | collective-permute-start | bytes 1769480 | tf_op jit(solution)/shard_map/ppermute | solution.py:10
  56.7 68.3 %all-gather.12.cloned.1.call-start = ((), (), s32[]{:S(2)}) async-start(), calls=%async_computation.2 | async-start | bytes 1769472 | tf_op jit(solution)/shard_map/all_gather | solution.py:46
  72.3 17.7 %collective-permute-start.2 = (bf16[768,384]{1,0:T(8,128)(2,1)}, bf16[768,384]{1,0:T(8,128)(2,1)}, u32[]{:S(2)}, u32[]{:S(2)}) collective-permute-start(bf16[768,384]{1,0:T(8,128)(2,1)} %get-tuple-element.4), channel_id=1, source_target_pairs={{4,0},{6,2},{8,4},{10,6},{12,8},{14,10},{16,12},{18,14},{20,16},{2... | collective-permute-start | bytes 1769480 | tf_op jit(solution)/shard_map/ppermute | solution.py:10
  73.6 30.2 %collective-permute-start.1 = (bf16[768,768]{1,0:T(8,128)(2,1)S(1)}, bf16[768,768]{1,0:T(8,128)(2,1)}, u32[]{:S(2)}, u32[]{:S(2)}) collective-permute-start(bf16[768,768]{1,0:T(8,128)(2,1)S(1)} %bitcast.52), channel_id=1, source_target_pairs={{2,0},{4,2},{6,4},{8,6},{10,8},{12,10},{14,12},{16,14},{18,16},{20... | collective-permute-start | bytes 3538952 | tf_op jit(solution)/shard_map/ppermute | solution.py:10
  90.1 82.1 %all-gather.14.cloned.1.call-start = ((), (), s32[]{:S(2)}) async-start(), calls=%async_computation.3 | async-start | bytes 1769472 | tf_op jit(solution)/shard_map/all_gather | solution.py:46
  107.2 53.4 %collective-permute-start.3 = (bf16[768,768]{1,0:T(8,128)(2,1)}, bf16[768,768]{1,0:T(8,128)(2,1)}, u32[]{:S(2)}, u32[]{:S(2)}) collective-permute-start(bf16[768,768]{1,0:T(8,128)(2,1)} %fusion), channel_id=1, source_target_pairs={{4,0},{6,2},{8,4},{10,6},{12,8},{14,10},{16,12},{18,14},{20,16},{2... | collective-permute-start | bytes 3538952 | tf_op jit(solution)/shard_map/ppermute | solution.py:10
  129.6 30.2 %collective-permute-start.4 = (bf16[768,384]{1,0:T(8,128)(2,1)S(1)}, bf16[768,384]{1,0:T(8,128)(2,1)S(1)}, u32[]{:S(2)}, u32[]{:S(2)}) collective-permute-start(bf16[768,384]{1,0:T(8,128)(2,1)S(1)} %get-tuple-element.6), channel_id=1, source_target_pairs={{8,0},{10,2},{12,4},{14,6},{16,8},{18,10},{20,12},{22,14},{24,16},... | collective-permute-start | bytes 1769480 | tf_op jit(solution)/shard_map/ppermute | solution.py:10
  159.7 0.8 copy-start.5
  160.6 113.1 %all-gather.16.cloned.1.call-start = ((), (), s32[]{:S(2)}) async-start(), calls=%async_computation.4 | async-start | bytes 1769472 | tf_op jit(solution)/shard_map/all_gather | solution.py:46
  164.7 29.7 %collective-permute-start.5 = (bf16[768,768]{1,0:T(8,128)(2,1)}, bf16[768,768]{1,0:T(8,128)(2,1)}, u32[]{:S(2)}, u32[]{:S(2)}) collective-permute-start(bf16[768,768]{1,0:T(8,128)(2,1)} %fusion.1), channel_id=1, source_target_pairs={{8,0},{10,2},{12,4},{14,6},{16,8},{18,10},{20,12},{22,14},{24,16},... | collective-permute-start | bytes 3538952 | tf_op jit(solution)/shard_map/ppermute | solution.py:10
  176.8 70.4 %collective-permute-start.6 = (bf16[768,384]{1,0:T(8,128)(2,1)S(1)}, bf16[768,384]{1,0:T(8,128)(2,1)S(1)}, u32[]{:S(2)}, u32[]{:S(2)}) collective-permute-start(bf16[768,384]{1,0:T(8,128)(2,1)S(1)} %get-tuple-element.8), channel_id=1, source_target_pairs={{16,0},{18,2},{20,4},{22,6},{24,8},{26,10},{28,12},{30,14},{17,1},... | collective-permute-start | bytes 1769480 | tf_op jit(solution)/shard_map/ppermute | solution.py:10
  198.5 72.0 %collective-permute-start.7 = (bf16[768,768]{1,0:T(8,128)(2,1)}, bf16[768,768]{1,0:T(8,128)(2,1)}, u32[]{:S(2)}, u32[]{:S(2)}) collective-permute-start(bf16[768,768]{1,0:T(8,128)(2,1)} %fusion.2), channel_id=1, source_target_pairs={{16,0},{18,2},{20,4},{22,6},{24,8},{26,10},{28,12},{30,14},{17,1},... | collective-permute-start | bytes 3538952 | tf_op jit(solution)/shard_map/ppermute | solution.py:10
  247.2 0.8 copy-start.4
  248.0 25.6 %copy-start.6 = (f32[768,384]{1,0:T(8,128)S(1)}, f32[768,384]{1,0:T(8,128)}, u32[]{:S(2)}) copy-start(f32[768,384]{1,0:T(8,128)} %get-tuple-element.9) | copy-start | bytes 3538948
Sparse Core Ops, SparseCore 0:
  10.1 11.8 all-gather.7
  23.6 10.3 all-gather.17
  56.8 11.2 all-gather.9
  90.2 34.7 all-gather.11
  160.7 11.4 all-gather.13
  248.2 9.6 all-gather.15
where the time goes:
time: 287 us; the launch traced here: 285 us
  waiting for transfers between devices  209 us (73%)
  matrix products  46 us (16%)
  between operations  14.3 us (5%)
  starting transfers between devices  10.7 us (4%)
  other arithmetic  3.21 us (1%)
    ppermute x8, waiting for transfers between devices, passed_along(): return lax.ppermute(block, axis, route)  160 us
    all_gather x4, waiting for transfers between devices, shards(): partner_cov = lax.all_gather(incoming, 'panel', axis=1, tiled=True)  33.9 us
    dot_general x4, matrix products, shards(): lax.dot_general(composite, middle, (((0,), (0,)), ((), ())), preferred_el...  17.6 us
    dot_general x3, matrix products, shards(): jnp.dot(partner_comp, composite, preferred_element_type=jnp.float32)  11.6 us
    ppermute x8, starting transfers between devices, passed_along(): return lax.ppermute(block, axis, route)  10.4 us
    all_gather x1, waiting for transfers between devices, shards(): full_coupling = lax.all_gather(own_part, 'panel', axis=1, tiled=True)  7.59 us
    all_gather x1, waiting for transfers between devices, shards(): lax.all_gather(factor_cols.astype(jnp.bfloat16), 'panel', axis=1, tiled=T...  7.26 us
  transfers between devices with their start and end apart: 14, of which 12 were waited for; matrix products, arithmetic and copies ran while one was open for 12% of the time, Pallas kernels for 0%

commit v1 on v0

v1 whole, which is shorter than its diff:
```python
import functools

import jax
import jax.numpy as jnp
from jax import lax
from jax.experimental import pallas as pl
from jax.experimental.pallas import tpu as pltpu
from jax.sharding import PartitionSpec as P

BF = jnp.bfloat16
F32 = jnp.float32
GROUP = 4
ANY = pl.BlockSpec(memory_space=pl.ANY)
VMEM = pl.BlockSpec(memory_space=pltpu.VMEM)
MIB = 1 << 20


def mm(a, b):
    return jnp.dot(a, b, preferred_element_type=F32)


def mm_t(a, b):
    return lax.dot_general(a, b, (((0,), (0,)), ((), ())), preferred_element_type=F32)


def whole(ref):
    return jnp.concatenate([ref[p] for p in range(ref.shape[0])], axis=1)


def put(ref, value):
    width = ref.shape[2]
    for p in range(ref.shape[0]):
        ref[p] = value[:, p * width : (p + 1) * width].astype(ref.dtype)


def where_am_i():
    t = lax.axis_index("tm")
    return t // GROUP, lax.rem(t, GROUP), lax.axis_index("panel")


def run(copies):
    for c in copies:
        c.start()
    for c in copies:
        c.wait()


def copy_all(pairs, sems):
    return [pltpu.make_async_copy(s, d, sems.at[i]) for i, (s, d) in enumerate(pairs)]


def panel_pairs(pieces, dst, q):
    n = len(pieces)
    return [(piece, dst.at[lax.rem(q + r, n)]) for r, piece in enumerate(pieces)]


def group_pairs(own, first, second, diag, dst, lo, q):
    n = len(own)
    pairs = []
    for r in range(n):
        p = lax.rem(q + r, n)
        even = 1 - lax.rem(p, 2)
        near, far = 1 + even, 2 - even
        for mask, piece in ((0, own[r]), (near, first[r]), (far, second[r]), (3, diag[r])):
            slot = jnp.bitwise_xor(lo, mask)
            pairs.append((piece, dst.at[slot, p]))
    return pairs


def split(refs, *counts):
    out, at = [], 0
    for c in counts:
        out.append(refs[at : at + c])
        at += c
    return out


def call(kernel, ins, in_specs, outs, scratch, flops):
    size = sum(a.size * a.dtype.itemsize for a in ins) + sum(
        o.size * o.dtype.itemsize for o in outs
    )
    return pl.pallas_call(
        kernel,
        in_specs=in_specs,
        out_specs=[VMEM] * len(outs),
        out_shape=outs,
        scratch_shapes=scratch,
        compiler_params=pltpu.CompilerParams(vmem_limit_bytes=36 * MIB),
        cost_estimate=pl.CostEstimate(flops=flops, bytes_accessed=size, transcendentals=0),
    )(*ins)


def base_kernel(n, *refs):
    factor, sigma, f_parts, c_parts, (base, base_bf), (f_all, c_all, sig, sems) = split(
        refs, 1, 1, n, n, 2, 4
    )
    factor, sigma = factor[0], sigma[0]
    hi, lo, q = where_am_i()
    width = factor.shape[1]
    run(copy_all(panel_pairs(f_parts, f_all, q), sems))
    own = factor[...]
    high = own.astype(BF)
    low = (own - high.astype(F32)).astype(BF)
    for p in range(n):
        part = f_all[p]
        base[p * width : (p + 1) * width, :] = mm_t(part, high) + mm_t(part, low)

    @pl.when(lax.axis_index("tm") == lax.axis_size("tm") - 1)
    def _():
        run(copy_all(panel_pairs(c_parts, c_all, q) + [(sigma, sig)], sems))
        s = sig[...]
        s_high = s.astype(BF)
        s_low = (s - s_high.astype(F32)).astype(BF)
        c_own = c_all[q]
        mid = mm(s_high, c_own) + mm(s_low, c_own)
        mid_high = mid.astype(BF)
        mid_low = (mid - mid_high.astype(F32)).astype(BF)
        c_full = whole(c_all)
        base[...] += mm_t(c_full, mid_high) + mm_t(c_full, mid_low)

    base_bf[...] = base[...].astype(BF)


def group_comp_kernel(n, *refs):
    own, first, second, diag, outs, (sems,) = split(refs, n, n, n, n, 5, 1)
    c, c01_ref, mine, agg, agg_panel = outs
    hi, lo, q = where_am_i()
    run(copy_all(group_pairs(own, first, second, diag, c, lo, q), sems))
    c01 = mm(whole(c.at[1]), whole(c.at[0])).astype(BF)
    put(c01_ref, c01)
    c23 = mm(whole(c.at[3]), whole(c.at[2])).astype(BF)
    put(agg, mm(c23, c01).astype(BF))
    agg_panel[...] = agg[q]

    @pl.when(lo == 0)
    def _():
        mine[...] = agg[...]

    @pl.when(lo == 1)
    def _():
        put(mine, mm(c23, whole(c.at[1])))

    @pl.when(lo == 2)
    def _():
        put(mine, c23)

    @pl.when(lo == 3)
    def _():
        mine[...] = c[3]


def sandwich(cov, comp_ref, q):
    mid = mm(cov, comp_ref[q]).astype(BF)
    return mm_t(whole(comp_ref), mid)


def group_cov_kernel(n, *refs):
    base, c, c01, own, first, second, diag, outs, scratch = split(
        refs, 1, 1, 1, n, n, n, n, 3, 3
    )
    base, c, c01 = base[0], c[0], c01[0]
    mine, agg, agg_bf = outs
    s, s23, sems = scratch
    hi, lo, q = where_am_i()
    run(copy_all(group_pairs(own, first, second, diag, s, lo, q), sems))
    c2 = whole(c.at[2])
    mid = mm(whole(s.at[3]), c2).astype(BF)
    put(s23, whole(s.at[2]).astype(F32) + mm_t(c2, mid))
    v23 = whole(s23)
    agg[...] = s[0, q].astype(F32)

    @pl.when(lo == 0)
    def _():
        agg[...] = base[...]

    agg[...] += sandwich(whole(s.at[1]), c.at[0], q)
    agg[...] += sandwich(v23, c01, q)
    agg_bf[...] = agg[...].astype(BF)

    @pl.when(lo == 0)
    def _():
        mine[...] = agg[...]

    @pl.when(lo == 1)
    def _():
        mine[...] = base[...] + sandwich(v23, c.at[1], q)

    @pl.when(lo == 2)
    def _():
        mine[...] = base[...] + sandwich(whole(s.at[3]), c.at[2], q)

    @pl.when(lo == 3)
    def _():
        mine[...] = base[...]


def receives(bit):
    hi, lo, q = where_am_i()
    return lax.rem(hi // (1 << bit), 2) == 0


def level_comp_kernel(n, bit, *refs):
    mine, agg, parts, outs, (got, sems) = split(refs, 1, 1, n, 3, 2)
    mine, agg = mine[0], agg[0]
    new_mine, new_agg, new_agg_panel = outs
    hi, lo, q = where_am_i()
    active = receives(bit)

    @pl.when(active)
    def _():
        run(copy_all(panel_pairs(parts, got, q), sems))
        c = whole(got)
        put(new_mine, mm(c, whole(mine)))
        put(new_agg, mm(c, whole(agg)))

    @pl.when(jnp.logical_not(active))
    def _():
        new_mine[...] = mine[...]
        new_agg[...] = agg[...]

    new_agg_panel[...] = new_agg[q]


def last_comp_kernel(n, bit, *refs):
    mine, parts, (out,), (got, sems) = split(refs, 1, n, 1, 2)
    mine = mine[0]
    hi, lo, q = where_am_i()
    active = receives(bit)

    @pl.when(active)
    def _():
        run(copy_all(panel_pairs(parts, got, q), sems))
        out[0] = mm(whole(got), mine[q]).astype(BF)

    @pl.when(jnp.logical_not(active))
    def _():
        out[0] = mine[q]


def level_cov_kernel(n, bit, *refs):
    cov, agg, mine_c, agg_c, parts, outs, (got, sems) = split(refs, 1, 1, 1, 1, n, 3, 2)
    cov, agg, mine_c, agg_c = cov[0], agg[0], mine_c[0], agg_c[0]
    new_cov, new_agg, new_agg_bf = outs
    hi, lo, q = where_am_i()
    active = receives(bit)
    new_cov[...] = cov[...]
    new_agg[...] = agg[...]

    @pl.when(active)
    def _():
        run(copy_all(panel_pairs(parts, got, q), sems))
        s = whole(got)
        new_cov[...] += sandwich(s, mine_c, q)
        new_agg[...] += sandwich(s, agg_c, q)

    new_agg_bf[...] = new_agg[...].astype(BF)


def last_cov_kernel(n, bit, *refs):
    cov, mine_c, parts, (out,), (got, sems) = split(refs, 1, 1, n, 1, 2)
    cov, mine_c = cov[0], mine_c[0]
    hi, lo, q = where_am_i()
    out[0] = cov[...]

    @pl.when(receives(bit))
    def _():
        run(copy_all(panel_pairs(parts, got, q), sems))
        out[0] += sandwich(whole(got), mine_c, q)


def over_panels(x):
    n = lax.axis_size("panel")
    return [x] + [
        lax.ppermute(x, "panel", [((i + r) % n, i) for i in range(n)]) for r in range(1, n)
    ]


def over_group(x):
    steps, n = lax.axis_size("tm"), lax.axis_size("panel")

    def swap(value, odd_mask, even_mask):
        pairs = []
        for t in range(steps):
            for q in range(n):
                mask = odd_mask if q % 2 else even_mask
                pairs.append((t * n + q, (t ^ mask) * n + q))
        return lax.ppermute(value, ("tm", "panel"), pairs)

    first = swap(x, 1, 2)
    second = swap(x, 2, 1)
    diag = swap(first, 2, 1)
    return [over_panels(v) for v in (x, first, second, diag)]


def to_receivers(x, bit):
    steps = lax.axis_size("tm")
    d = 1 << bit
    got = None
    t = lax.axis_index("tm") // GROUP
    for back in range(1, d + 1):
        pairs = [
            (g * GROUP + k, (g - back) * GROUP + k)
            for g in range(d, steps // GROUP, 2 * d)
            for k in range(GROUP)
        ]
        here = lax.ppermute(x, "tm", pairs)
        got = here if got is None else jnp.where(lax.rem(t, d) == d - back, here, got)
    return over_panels(got)


def shards(factor_inverse, coupling, sigma_after):
    steps = lax.axis_size("tm")
    n = lax.axis_size("panel")
    nb, w = factor_inverse.shape[1:]
    levels = (steps // GROUP - 1).bit_length()
    panel_bf = jax.ShapeDtypeStruct((nb, w), BF)
    panel_f32 = jax.ShapeDtypeStruct((nb, w), F32)
    full_bf = jax.ShapeDtypeStruct((n, nb, w), BF)
    group_bf = jax.ShapeDtypeStruct((GROUP, n, nb, w), BF)
    one = 2 * nb * nb * w
    sems = pltpu.SemaphoreType.DMA

    comp = coupling[0].astype(BF)
    c_group = over_group(comp)
    factor = factor_inverse[0]
    f_parts = over_panels(factor.astype(BF))
    base, base_bf = call(
        functools.partial(base_kernel, n),
        [factor, sigma_after, *f_parts, *c_group[0]],
        [VMEM] + [ANY] * (1 + 2 * n),
        [panel_f32, panel_bf],
        [
            pltpu.VMEM((n, nb, w), BF),
            pltpu.VMEM((n, nb, w), BF),
            pltpu.VMEM((nb, n * w), F32),
            sems((n + 1,)),
        ],
        2 * one,
    )
    s_group = over_group(base_bf)
    pieces = [p for block in c_group for p in block]
    c_all, c01, mine_c, agg_c, agg_c_panel = call(
        functools.partial(group_comp_kernel, n),
        pieces,
        [ANY] * len(pieces),
        [group_bf, full_bf, full_bf, full_bf, panel_bf],
        [sems((GROUP * n,))],
        4 * n * one,
    )
    pieces = [p for block in s_group for p in block]
    cov, agg, agg_bf = call(
        functools.partial(group_cov_kernel, n),
        [base, c_all, c01, *pieces],
        [VMEM] * 3 + [ANY] * len(pieces),
        [panel_f32, panel_f32, panel_bf],
        [pltpu.VMEM((GROUP, n, nb, w), BF), pltpu.VMEM((n, nb, w), BF), sems((GROUP * n,))],
        (2 * n + 6) * one,
    )
    out_cov = jax.ShapeDtypeStruct((1, nb, w), F32)
    out_comp = jax.ShapeDtypeStruct((1, nb, w), BF)
    scratch = [pltpu.VMEM((n, nb, w), BF), sems((n,))]
    for bit in range(levels):
        c_parts = to_receivers(agg_c_panel, bit)
        s_parts = to_receivers(agg_bf, bit)
        if bit + 1 < levels:
            new_mine_c, new_agg_c, agg_c_panel = call(
                functools.partial(level_comp_kernel, n, bit),
                [mine_c, agg_c, *c_parts],
                [VMEM] * 2 + [ANY] * n,
                [full_bf, full_bf, panel_bf],
                scratch,
                2 * n * one,
            )
            cov, agg, agg_bf = call(
                functools.partial(level_cov_kernel, n, bit),
                [cov, agg, mine_c, agg_c, *s_parts],
                [VMEM] * 4 + [ANY] * n,
                [panel_f32, panel_f32, panel_bf],
                scratch,
                4 * one,
            )
            mine_c, agg_c = new_mine_c, new_agg_c
        else:
            (prop,) = call(
                functools.partial(last_comp_kernel, n, bit),
                [mine_c, *c_parts],
                [VMEM] + [ANY] * n,
                [out_comp],
                scratch,
                one,
            )
            (cov,) = call(
                functools.partial(last_cov_kernel, n, bit),
                [cov, mine_c, *s_parts],
                [VMEM] * 2 + [ANY] * n,
                [out_cov],
                scratch,
                2 * one,
            )
    return cov, prop


def solution(mesh):
    placed = (P("tm", None, "panel"), P("tm", None, "panel"), P())
    return jax.shard_map(
        shards,
        mesh=mesh,
        in_specs=placed,
        out_specs=(P("tm", None, "panel"), P("tm", None, "panel")),
        check_vma=False,
    )
```

time: 287 us -> 146 us (0.51)
  the two profiles are of different devices: /device:TPU:0 before, /device:TPU:11 now
where the time goes in v1:
time: 146 us
  waiting for transfers between devices  92.8 us (64%)
  starting transfers between devices  25.4 us (17%)
  Pallas kernels  21.6 us (15%)
  other arithmetic  5.1 us (3%)
    ppermute x6, waiting for transfers between devices, to_receivers(): here = lax.ppermute(x, 'tm', pairs)  65 us
    ppermute x6, waiting for transfers between devices, swap(): return lax.ppermute(value, ('tm', 'panel'), pairs)  27.4 us
    pallas_call x7, Pallas kernels, call(): pl.pallas_call(kernel, in_specs=in_specs, out_specs=[VMEM] * len(outs), o...  21.6 us
    ppermute x13, starting transfers between devices, over_panels(): lax.ppermute(x, 'panel', [((i + r) % n, i) for i in range(n)])  10.3 us
    ppermute x6, starting transfers between devices, to_receivers(): here = lax.ppermute(x, 'tm', pairs)  8.96 us
    ppermute x6, starting transfers between devices, swap(): return lax.ppermute(value, ('tm', 'panel'), pairs)  6.11 us
  transfers between devices with their start and end apart: 25, of which 10 were waited for; matrix products, arithmetic and copies ran while one was open for 2% of the time, Pallas kernels for 13%

profile of v1, /device:TPU:11, one launch (start us, length us, event | category | flops | bytes accessed | tf_op | source)
XLA Modules:
  0.0 145.9 jit_solution(4199962795291681284)
XLA Ops:
  0.6 1.5 %bitcast_convert_fusion.refs_2_ = bf16[768,384]{1,0:T(8,128)(2,1)S(1)} fusion(f32[1,768,384]{2,1,0:T(8,128)} %param.3), kind=kLoop, calls=%fused_computation.3 | loop fusion | flops 294912 | bytes 1769472 | tf_op jit(solution)/shard_map/convert_element_type | solution.py:326
  2.9 1.3 convert_bitcast_fusion.refs_4_.refs_0_
  4.6 1.2 collective-permute-start.4
  6.3 1.8 %shard_map.50 = (f32[768,384]{1,0:T(8,128)S(1)}, bf16[768,384]{1,0:T(8,128)(2,1)S(1)}) custom-call(f32[768,384]{1,0:T(8,128)S(1)} %bitcast.4, f32[768,768]{1,0:T(8,128)S(1)} %copy-done.1, bf16[768,384]{1,0:T(8,128)(2,1)S(1)} %bitcast_convert_fusion.refs_2_, bf16[768,384]{1,0:T(8,128)(2,1)S(1)} %collective-permute-done.refs_3_, ...), custom_call_target="tpu_custom_call" | custom-call | flops 905969664 | bytes 7667712 | tf_op jit(solution)/shard_map/pallas_call | solution.py:82
  9.0 8.3 %collective-permute-done.2.refs_2_ = bf16[768,384]{1,0:T(8,128)(2,1)S(1)} collective-permute-done((bf16[768,384]{1,0:T(8,128)(2,1)S(1)}, bf16[768,384]{1,0:T(8,128)(2,1)S(1)}, u32[]{:S(2)}, u32[]{:S(2)}) %collective-permute-start.2) | collective-permute-done | bytes 589856 | tf_op jit(solution)/shard_map/ppermute | solution.py:287
  17.3 2.3 %collective-permute-start.6 = (bf16[768,384]{1,0:T(8,128)(2,1)S(1)}, bf16[768,384]{1,0:T(8,128)(2,1)S(1)}, u32[]{:S(2)}, u32[]{:S(2)}) collective-permute-start(bf16[768,384]{1,0:T(8,128)(2,1)S(1)} %collective-permute-done.2.refs_2_), channel_id=1, source_target_pairs={{0,2},{1,5},{2,0},{3,7},{4,6},{5,1},{6,4},{7,3},{8,10},{9,13},{10,... | collective-permute-start | bytes 1769480 | tf_op jit(solution)/shard_map/ppermute | solution.py:287
  19.5 1.7 %collective-permute-start.3 = (bf16[768,384]{1,0:T(8,128)(2,1)S(1)}, bf16[768,384]{1,0:T(8,128)(2,1)S(1)}, u32[]{:S(2)}, u32[]{:S(2)}) collective-permute-start(bf16[768,384]{1,0:T(8,128)(2,1)S(1)} %collective-permute-done.2.refs_2_), channel_id=1, source_target_pairs={{1,0},{0,1},{3,2},{2,3},{5,4},{4,5},{7,6},{6,7},{9,8},{8,9},{11,10... | collective-permute-start | bytes 1769480 | tf_op jit(solution)/shard_map/ppermute | solution.py:274
  21.2 1.4 collective-permute-start.5
  22.8 5.7 %collective-permute-done.9.refs_5_ = bf16[768,384]{1,0:T(8,128)(2,1)S(1)} collective-permute-done((bf16[768,384]{1,0:T(8,128)(2,1)S(1)}, bf16[768,384]{1,0:T(8,128)(2,1)S(1)}, u32[]{:S(2)}, u32[]{:S(2)}) %collective-permute-start.9) | collective-permute-done | bytes 589856 | tf_op jit(solution)/shard_map/ppermute | solution.py:287
  28.5 1.2 collective-permute-start.13
  29.7 2.9 %collective-permute-done.6.refs_6_ = bf16[768,384]{1,0:T(8,128)(2,1)S(1)} collective-permute-done((bf16[768,384]{1,0:T(8,128)(2,1)S(1)}, bf16[768,384]{1,0:T(8,128)(2,1)S(1)}, u32[]{:S(2)}, u32[]{:S(2)}) %collective-permute-start.6) | collective-permute-done | bytes 589856 | tf_op jit(solution)/shard_map/ppermute | solution.py:287
  32.6 1.2 collective-permute-start.7
  34.4 4.6 %collective-permute-done.11.refs_7_ = bf16[768,384]{1,0:T(8,128)(2,1)S(1)} collective-permute-done((bf16[768,384]{1,0:T(8,128)(2,1)S(1)}, bf16[768,384]{1,0:T(8,128)(2,1)S(1)}, u32[]{:S(2)}, u32[]{:S(2)}) %collective-permute-start.11) | collective-permute-done | bytes 589856 | tf_op jit(solution)/shard_map/ppermute | solution.py:287
  39.1 5.9 %collective-permute-done.13.refs_9_ = bf16[768,384]{1,0:T(8,128)(2,1)S(1)} collective-permute-done((bf16[768,384]{1,0:T(8,128)(2,1)S(1)}, bf16[768,384]{1,0:T(8,128)(2,1)S(1)}, u32[]{:S(2)}, u32[]{:S(2)}) %collective-permute-start.13) | collective-permute-done | bytes 589856 | tf_op jit(solution)/shard_map/ppermute | solution.py:287
  45.4 5.4 %shard_map.51 = (bf16[4,2,768,384]{3,2,1,0:T(8,128)(2,1)S(1)}, bf16[2,768,384]{2,1,0:T(8,128)(2,1)S(1)}, bf16[2,768,384]{2,1,0:T(8,128)(2,1)S(1)}, bf16[2,768,384]{2,1,0:T(8,128)(2,1)S(1)}, bf16[768,384]{1,0:T(8,128)(2,1)S(1)}) custom-call(bf16[768,384]{1,0:T(8,128)(2,1)S(1)} %convert_bitcast_fusion.refs_4_.refs_0_, ...), custom_call_target="tpu_custom_call" | custom-call | flops 3623878656 | bytes 13565952 | tf_op jit(solution)/shard_map/pallas_call | solution.py:82
  50.8 2.1 %collective-permute-start.17 = (bf16[768,384]{1,0:T(8,128)(2,1)S(1)}, bf16[768,384]{1,0:T(8,128)(2,1)S(1)}, u32[]{:S(2)}, u32[]{:S(2)}) collective-permute-start(bf16[768,384]{1,0:T(8,128)(2,1)S(1)} %get-tuple-element.26), channel_id=1, source_target_pairs={{8,0},{10,2},{12,4},{14,6},{24,16},{26,18},{28,20},{30,22},{9,1},{... | collective-permute-start | bytes 1769480 | tf_op jit(solution)/shard_map/ppermute | solution.py:306
  53.0 7.4 %shard_map.52 = (f32[768,384]{1,0:T(8,128)S(1)}, f32[768,384]{1,0:T(8,128)S(1)}, bf16[768,384]{1,0:T(8,128)(2,1)S(1)}) custom-call(f32[768,384]{1,0:T(8,128)S(1)} %get-tuple-element.16.refs_0_, bf16[4,2,768,384]{3,2,1,0:T(8,128)(2,1)S(1)} %get-tuple-element.17.refs_1_, bf16[2,768,384]{2,1,0:T(8,128)(2,1)S(1)} %get-tuple-element.18.refs_2_, ...), custom_call_target="tpu_custom_call" | custom-call | flops 4529848320 | bytes 14745600 | tf_op jit(solution)/shard_map/pallas_call | solution.py:82
  60.4 1.3 collective-permute-start.15
  61.7 3.9 %collective-permute-done.17.refs_2_ = bf16[768,384]{1,0:T(8,128)(2,1)S(1)} collective-permute-done((bf16[768,384]{1,0:T(8,128)(2,1)S(1)}, bf16[768,384]{1,0:T(8,128)(2,1)S(1)}, u32[]{:S(2)}, u32[]{:S(2)}) %collective-permute-start.17) | collective-permute-done | bytes 589856 | tf_op jit(solution)/shard_map/ppermute | solution.py:306
  65.6 1.2 collective-permute-start.18
  66.9 11.4 %collective-permute-done.15.refs_4_ = bf16[768,384]{1,0:T(8,128)(2,1)S(1)} collective-permute-done((bf16[768,384]{1,0:T(8,128)(2,1)S(1)}, bf16[768,384]{1,0:T(8,128)(2,1)S(1)}, u32[]{:S(2)}, u32[]{:S(2)}) %collective-permute-start.15) | collective-permute-done | bytes 589856 | tf_op jit(solution)/shard_map/ppermute | solution.py:306
  79.1 1.2 shard_map.54
  80.3 1.5 %collective-permute-start.22 = (bf16[768,384]{1,0:T(8,128)(2,1)S(1)}, bf16[768,384]{1,0:T(8,128)(2,1)}, u32[]{:S(2)}, u32[]{:S(2)}) collective-permute-start(bf16[768,384]{1,0:T(8,128)(2,1)S(1)} %get-tuple-element.29), channel_id=1, source_target_pairs={{16,0},{18,2},{20,4},{22,6},{17,1},{19,3},{21,5},{23,7}} | collective-permute-start | bytes 1769480 | tf_op jit(solution)/shard_map/ppermute | solution.py:306
  81.8 1.3 collective-permute-start.23
  83.1 1.2 shard_map.53
  84.3 1.5 %collective-permute-start.19 = (bf16[768,384]{1,0:T(8,128)(2,1)S(1)}, bf16[768,384]{1,0:T(8,128)(2,1)}, u32[]{:S(2)}, u32[]{:S(2)}) collective-permute-start(bf16[768,384]{1,0:T(8,128)(2,1)S(1)} %get-tuple-element.28), channel_id=1, source_target_pairs={{16,0},{18,2},{20,4},{22,6},{17,1},{19,3},{21,5},{23,7}} | collective-permute-start | bytes 1769480 | tf_op jit(solution)/shard_map/ppermute | solution.py:306
  85.8 1.3 collective-permute-start.20
  87.1 26.8 %collective-permute-done.23 = bf16[768,384]{1,0:T(8,128)(2,1)} collective-permute-done((bf16[768,384]{1,0:T(8,128)(2,1)S(1)}, bf16[768,384]{1,0:T(8,128)(2,1)}, u32[]{:S(2)}, u32[]{:S(2)}) %collective-permute-start.23) | collective-permute-done | bytes 589856 | tf_op jit(solution)/shard_map/ppermute | solution.py:306
  115.0 1.2 collective-permute-start.24
  116.2 22.9 %collective-permute-done.20 = bf16[768,384]{1,0:T(8,128)(2,1)} collective-permute-done((bf16[768,384]{1,0:T(8,128)(2,1)S(1)}, bf16[768,384]{1,0:T(8,128)(2,1)}, u32[]{:S(2)}, u32[]{:S(2)}) %collective-permute-start.20) | collective-permute-done | bytes 589856 | tf_op jit(solution)/shard_map/ppermute | solution.py:306
  141.1 1.8 %shard_map.56 = bf16[1,768,384]{2,1,0:T(8,128)(2,1)} custom-call(bf16[2,768,384]{2,1,0:T(8,128)(2,1)S(1)} %get-tuple-element.27.refs_1_.refs_0_, bf16[768,384]{1,0:T(8,128)(2,1)S(1)} %broadcast_select_fusion.refs_1_, bf16[768,384]{1,0:T(8,128)(2,1)S(1)} %collective-permute-done.24.refs_2_), custom_call_target="tpu_custom_call" | custom-call | flops 452984832 | bytes 2949120 | tf_op jit(solution)/shard_map/pallas_call | solution.py:82
  143.0 2.7 %shard_map.55 = f32[1,768,384]{2,1,0:T(8,128)} custom-call(f32[768,384]{1,0:T(8,128)S(1)} %get-tuple-element.25.refs_0_, bf16[2,768,384]{2,1,0:T(8,128)(2,1)S(1)} %get-tuple-element.27.refs_1_.refs_0_, bf16[768,384]{1,0:T(8,128)(2,1)S(1)} %broadcast_select_fusion.1.refs_2_, bf16[768,384]{1,0:T(8,128)(2,1)S(1)} %collective-permute-done.21.refs_3_), custom_call_target="tpu_custom_call" | custom-call | flops 905969664 | bytes 4718592 | tf_op jit(solution)/shard_map/pallas_call | solution.py:82
  (33 shorter events, 7.7 us)
Async XLA Ops:
  0.6 5.7 %copy-start.1 = (f32[768,768]{1,0:T(8,128)S(1)}, f32[768,768]{1,0:T(8,128)}, u32[]{:S(2)}) copy-start(f32[768,768]{1,0:T(8,128)} %refs_1_.1) | copy-start | bytes 7077892
  2.1 4.2 %copy-start = (f32[1,768,384]{2,1,0:T(8,128)S(1)}, f32[1,768,384]{2,1,0:T(8,128)}, u32[]{:S(2)}) copy-start(f32[1,768,384]{2,1,0:T(8,128)} %param.3) | copy-start | bytes 3538948
  2.1 3.7 %collective-permute-start = (bf16[768,384]{1,0:T(8,128)(2,1)S(1)}, bf16[768,384]{1,0:T(8,128)(2,1)S(1)}, u32[]{:S(2)}, u32[]{:S(2)}) collective-permute-start(bf16[768,384]{1,0:T(8,128)(2,1)S(1)} %bitcast_convert_fusion.refs_2_), channel_id=1, source_target_pairs={{1,0},{0,1},{3,2},{2,3},{5,4},{4,5},{7,6},{6,7},{9,8},{8,9},{11,10... | collective-permute-start | bytes 1769480 | tf_op jit(solution)/shard_map/ppermute | solution.py:274
  4.2 2.1 %collective-permute-start.1 = (bf16[768,384]{1,0:T(8,128)(2,1)S(1)}, bf16[768,384]{1,0:T(8,128)(2,1)S(1)}, u32[]{:S(2)}, u32[]{:S(2)}) collective-permute-start(bf16[768,384]{1,0:T(8,128)(2,1)S(1)} %convert_bitcast_fusion.refs_4_.refs_0_), channel_id=1, source_target_pairs={{1,0},{0,1},{3,2},{2,3},{5,4},{4,5},{7,6},{6,7},{9,8},{8,9},{11,10... | collective-permute-start | bytes 1769480 | tf_op jit(solution)/shard_map/ppermute | solution.py:274
  4.4 12.9 %collective-permute-start.2 = (bf16[768,384]{1,0:T(8,128)(2,1)S(1)}, bf16[768,384]{1,0:T(8,128)(2,1)S(1)}, u32[]{:S(2)}, u32[]{:S(2)}) collective-permute-start(bf16[768,384]{1,0:T(8,128)(2,1)S(1)} %convert_bitcast_fusion.refs_4_.refs_0_), channel_id=1, source_target_pairs={{0,4},{1,3},{2,6},{3,1},{4,0},{5,7},{6,2},{7,5},{8,12},{9,11},{10,... | collective-permute-start | bytes 1769480 | tf_op jit(solution)/shard_map/ppermute | solution.py:287
  4.6 16.6 %collective-permute-start.4 = (bf16[768,384]{1,0:T(8,128)(2,1)S(1)}, bf16[768,384]{1,0:T(8,128)(2,1)S(1)}, u32[]{:S(2)}, u32[]{:S(2)}) collective-permute-start(bf16[768,384]{1,0:T(8,128)(2,1)S(1)} %convert_bitcast_fusion.refs_4_.refs_0_), channel_id=1, source_target_pairs={{0,2},{1,5},{2,0},{3,7},{4,6},{5,1},{6,4},{7,3},{8,10},{9,13},{10,... | collective-permute-start | bytes 1769480 | tf_op jit(solution)/shard_map/ppermute | solution.py:287
  8.1 20.4 %collective-permute-start.9 = (bf16[768,384]{1,0:T(8,128)(2,1)S(1)}, bf16[768,384]{1,0:T(8,128)(2,1)S(1)}, u32[]{:S(2)}, u32[]{:S(2)}) collective-permute-start(bf16[768,384]{1,0:T(8,128)(2,1)S(1)} %get-tuple-element.19.refs_3_), channel_id=1, source_target_pairs={{0,4},{1,3},{2,6},{3,1},{4,0},{5,7},{6,2},{7,5},{8,12},{9,11},{10,... | collective-permute-start | bytes 1769480 | tf_op jit(solution)/shard_map/ppermute | solution.py:287
  17.3 15.4 %collective-permute-start.6 = (bf16[768,384]{1,0:T(8,128)(2,1)S(1)}, bf16[768,384]{1,0:T(8,128)(2,1)S(1)}, u32[]{:S(2)}, u32[]{:S(2)}) collective-permute-start(bf16[768,384]{1,0:T(8,128)(2,1)S(1)} %collective-permute-done.2.refs_2_), channel_id=1, source_target_pairs={{0,2},{1,5},{2,0},{3,7},{4,6},{5,1},{6,4},{7,3},{8,10},{9,13},{10,... | collective-permute-start | bytes 1769480 | tf_op jit(solution)/shard_map/ppermute | solution.py:287
  19.5 14.3 %collective-permute-start.3 = (bf16[768,384]{1,0:T(8,128)(2,1)S(1)}, bf16[768,384]{1,0:T(8,128)(2,1)S(1)}, u32[]{:S(2)}, u32[]{:S(2)}) collective-permute-start(bf16[768,384]{1,0:T(8,128)(2,1)S(1)} %collective-permute-done.2.refs_2_), channel_id=1, source_target_pairs={{1,0},{0,1},{3,2},{2,3},{5,4},{4,5},{7,6},{6,7},{9,8},{8,9},{11,10... | collective-permute-start | bytes 1769480 | tf_op jit(solution)/shard_map/ppermute | solution.py:274
  21.2 12.7 %collective-permute-start.5 = (bf16[768,384]{1,0:T(8,128)(2,1)S(1)}, bf16[768,384]{1,0:T(8,128)(2,1)S(1)}, u32[]{:S(2)}, u32[]{:S(2)}) collective-permute-start(bf16[768,384]{1,0:T(8,128)(2,1)S(1)} %collective-permute-done.4.refs_4_), channel_id=1, source_target_pairs={{1,0},{0,1},{3,2},{2,3},{5,4},{4,5},{7,6},{6,7},{9,8},{8,9},{11,10... | collective-permute-start | bytes 1769480 | tf_op jit(solution)/shard_map/ppermute | solution.py:274
  22.6 16.4 %collective-permute-start.11 = (bf16[768,384]{1,0:T(8,128)(2,1)S(1)}, bf16[768,384]{1,0:T(8,128)(2,1)S(1)}, u32[]{:S(2)}, u32[]{:S(2)}) collective-permute-start(bf16[768,384]{1,0:T(8,128)(2,1)S(1)} %get-tuple-element.19.refs_3_), channel_id=1, source_target_pairs={{0,2},{1,5},{2,0},{3,7},{4,6},{5,1},{6,4},{7,3},{8,10},{9,13},{10,... | collective-permute-start | bytes 1769480 | tf_op jit(solution)/shard_map/ppermute | solution.py:287
  28.5 16.5 %collective-permute-start.13 = (bf16[768,384]{1,0:T(8,128)(2,1)S(1)}, bf16[768,384]{1,0:T(8,128)(2,1)S(1)}, u32[]{:S(2)}, u32[]{:S(2)}) collective-permute-start(bf16[768,384]{1,0:T(8,128)(2,1)S(1)} %collective-permute-done.9.refs_5_), channel_id=1, source_target_pairs={{0,2},{1,5},{2,0},{3,7},{4,6},{5,1},{6,4},{7,3},{8,10},{9,13},{10,... | collective-permute-start | bytes 1769480 | tf_op jit(solution)/shard_map/ppermute | solution.py:287
  32.6 12.8 %collective-permute-start.7 = (bf16[768,384]{1,0:T(8,128)(2,1)S(1)}, bf16[768,384]{1,0:T(8,128)(2,1)S(1)}, u32[]{:S(2)}, u32[]{:S(2)}) collective-permute-start(bf16[768,384]{1,0:T(8,128)(2,1)S(1)} %collective-permute-done.6.refs_6_), channel_id=1, source_target_pairs={{1,0},{0,1},{3,2},{2,3},{5,4},{4,5},{7,6},{6,7},{9,8},{8,9},{11,10... | collective-permute-start | bytes 1769480 | tf_op jit(solution)/shard_map/ppermute | solution.py:274
  33.8 19.1 %collective-permute-start.8 = (bf16[768,384]{1,0:T(8,128)(2,1)S(1)}, bf16[768,384]{1,0:T(8,128)(2,1)S(1)}, u32[]{:S(2)}, u32[]{:S(2)}) collective-permute-start(bf16[768,384]{1,0:T(8,128)(2,1)S(1)} %get-tuple-element.19.refs_3_), channel_id=1, source_target_pairs={{1,0},{0,1},{3,2},{2,3},{5,4},{4,5},{7,6},{6,7},{9,8},{8,9},{11,10... | collective-permute-start | bytes 1769480 | tf_op jit(solution)/shard_map/ppermute | solution.py:274
  33.9 19.0 %collective-permute-start.10 = (bf16[768,384]{1,0:T(8,128)(2,1)S(1)}, bf16[768,384]{1,0:T(8,128)(2,1)S(1)}, u32[]{:S(2)}, u32[]{:S(2)}) collective-permute-start(bf16[768,384]{1,0:T(8,128)(2,1)S(1)} %collective-permute-done.9.refs_5_), channel_id=1, source_target_pairs={{1,0},{0,1},{3,2},{2,3},{5,4},{4,5},{7,6},{6,7},{9,8},{8,9},{11,10... | collective-permute-start | bytes 1769480 | tf_op jit(solution)/shard_map/ppermute | solution.py:274
  38.9 14.0 %collective-permute-start.12 = (bf16[768,384]{1,0:T(8,128)(2,1)S(1)}, bf16[768,384]{1,0:T(8,128)(2,1)S(1)}, u32[]{:S(2)}, u32[]{:S(2)}) collective-permute-start(bf16[768,384]{1,0:T(8,128)(2,1)S(1)} %collective-permute-done.11.refs_7_), channel_id=1, source_target_pairs={{1,0},{0,1},{3,2},{2,3},{5,4},{4,5},{7,6},{6,7},{9,8},{8,9},{11,10... | collective-permute-start | bytes 1769480 | tf_op jit(solution)/shard_map/ppermute | solution.py:274
  45.0 8.0 %collective-permute-start.14 = (bf16[768,384]{1,0:T(8,128)(2,1)S(1)}, bf16[768,384]{1,0:T(8,128)(2,1)S(1)}, u32[]{:S(2)}, u32[]{:S(2)}) collective-permute-start(bf16[768,384]{1,0:T(8,128)(2,1)S(1)} %collective-permute-done.13.refs_9_), channel_id=1, source_target_pairs={{1,0},{0,1},{3,2},{2,3},{5,4},{4,5},{7,6},{6,7},{9,8},{8,9},{11,10... | collective-permute-start | bytes 1769480 | tf_op jit(solution)/shard_map/ppermute | solution.py:274
  50.8 14.8 %collective-permute-start.17 = (bf16[768,384]{1,0:T(8,128)(2,1)S(1)}, bf16[768,384]{1,0:T(8,128)(2,1)S(1)}, u32[]{:S(2)}, u32[]{:S(2)}) collective-permute-start(bf16[768,384]{1,0:T(8,128)(2,1)S(1)} %get-tuple-element.26), channel_id=1, source_target_pairs={{8,0},{10,2},{12,4},{14,6},{24,16},{26,18},{28,20},{30,22},{9,1},{... | collective-permute-start | bytes 1769480 | tf_op jit(solution)/shard_map/ppermute | solution.py:306
  60.4 17.9 %collective-permute-start.15 = (bf16[768,384]{1,0:T(8,128)(2,1)S(1)}, bf16[768,384]{1,0:T(8,128)(2,1)S(1)}, u32[]{:S(2)}, u32[]{:S(2)}) collective-permute-start(bf16[768,384]{1,0:T(8,128)(2,1)S(1)} %get-tuple-element.24), channel_id=1, source_target_pairs={{8,0},{10,2},{12,4},{14,6},{24,16},{26,18},{28,20},{30,22},{9,1},{... | collective-permute-start | bytes 1769480 | tf_op jit(solution)/shard_map/ppermute | solution.py:306
  65.6 13.5 %collective-permute-start.18 = (bf16[768,384]{1,0:T(8,128)(2,1)S(1)}, bf16[768,384]{1,0:T(8,128)(2,1)S(1)}, u32[]{:S(2)}, u32[]{:S(2)}) collective-permute-start(bf16[768,384]{1,0:T(8,128)(2,1)S(1)} %collective-permute-done.17.refs_2_), channel_id=1, source_target_pairs={{1,0},{0,1},{3,2},{2,3},{5,4},{4,5},{7,6},{6,7},{9,8},{8,9},{11,10... | collective-permute-start | bytes 1769480 | tf_op jit(solution)/shard_map/ppermute | solution.py:274
  78.3 4.8 %collective-permute-start.16 = (bf16[768,384]{1,0:T(8,128)(2,1)S(1)}, bf16[768,384]{1,0:T(8,128)(2,1)S(1)}, u32[]{:S(2)}, u32[]{:S(2)}) collective-permute-start(bf16[768,384]{1,0:T(8,128)(2,1)S(1)} %collective-permute-done.15.refs_4_), channel_id=1, source_target_pairs={{1,0},{0,1},{3,2},{2,3},{5,4},{4,5},{7,6},{6,7},{9,8},{8,9},{11,10... | collective-permute-start | bytes 1769480 | tf_op jit(solution)/shard_map/ppermute | solution.py:274
  80.3 6.8 %collective-permute-start.22 = (bf16[768,384]{1,0:T(8,128)(2,1)S(1)}, bf16[768,384]{1,0:T(8,128)(2,1)}, u32[]{:S(2)}, u32[]{:S(2)}) collective-permute-start(bf16[768,384]{1,0:T(8,128)(2,1)S(1)} %get-tuple-element.29), channel_id=1, source_target_pairs={{16,0},{18,2},{20,4},{22,6},{17,1},{19,3},{21,5},{23,7}} | collective-permute-start | bytes 1769480 | tf_op jit(solution)/shard_map/ppermute | solution.py:306
  81.8 32.1 %collective-permute-start.23 = (bf16[768,384]{1,0:T(8,128)(2,1)S(1)}, bf16[768,384]{1,0:T(8,128)(2,1)}, u32[]{:S(2)}, u32[]{:S(2)}) collective-permute-start(bf16[768,384]{1,0:T(8,128)(2,1)S(1)} %get-tuple-element.29), channel_id=1, source_target_pairs={{16,8},{18,10},{20,12},{22,14},{17,9},{19,11},{21,13},{23,15}} | collective-permute-start | bytes 1769480 | tf_op jit(solution)/shard_map/ppermute | solution.py:306
  84.3 31.9 %collective-permute-start.19 = (bf16[768,384]{1,0:T(8,128)(2,1)S(1)}, bf16[768,384]{1,0:T(8,128)(2,1)}, u32[]{:S(2)}, u32[]{:S(2)}) collective-permute-start(bf16[768,384]{1,0:T(8,128)(2,1)S(1)} %get-tuple-element.28), channel_id=1, source_target_pairs={{16,0},{18,2},{20,4},{22,6},{17,1},{19,3},{21,5},{23,7}} | collective-permute-start | bytes 1769480 | tf_op jit(solution)/shard_map/ppermute | solution.py:306
  85.8 53.4 %collective-permute-start.20 = (bf16[768,384]{1,0:T(8,128)(2,1)S(1)}, bf16[768,384]{1,0:T(8,128)(2,1)}, u32[]{:S(2)}, u32[]{:S(2)}) collective-permute-start(bf16[768,384]{1,0:T(8,128)(2,1)S(1)} %get-tuple-element.28), channel_id=1, source_target_pairs={{16,8},{18,10},{20,12},{22,14},{17,9},{19,11},{21,13},{23,15}} | collective-permute-start | bytes 1769480 | tf_op jit(solution)/shard_map/ppermute | solution.py:306
  115.0 26.1 %collective-permute-start.24 = (bf16[768,384]{1,0:T(8,128)(2,1)S(1)}, bf16[768,384]{1,0:T(8,128)(2,1)S(1)}, u32[]{:S(2)}, u32[]{:S(2)}) collective-permute-start(bf16[768,384]{1,0:T(8,128)(2,1)S(1)} %broadcast_select_fusion.refs_1_), channel_id=1, source_target_pairs={{1,0},{0,1},{3,2},{2,3},{5,4},{4,5},{7,6},{6,7},{9,8},{8,9},{11,10... | collective-permute-start | bytes 1769480 | tf_op jit(solution)/shard_map/ppermute | solution.py:274
  140.3 2.7 %collective-permute-start.21 = (bf16[768,384]{1,0:T(8,128)(2,1)S(1)}, bf16[768,384]{1,0:T(8,128)(2,1)S(1)}, u32[]{:S(2)}, u32[]{:S(2)}) collective-permute-start(bf16[768,384]{1,0:T(8,128)(2,1)S(1)} %broadcast_select_fusion.1.refs_2_), channel_id=1, source_target_pairs={{1,0},{0,1},{3,2},{2,3},{5,4},{4,5},{7,6},{6,7},{9,8},{8,9},{11,10... | collective-permute-start | bytes 1769480 | tf_op jit(solution)/shard_map/ppermute | solution.py:274
